TPU v7x, 512 devices: a whole 4x8x8 slice. The times are simulated.
512 devices in a mesh: fsdp: 64 (over z, x, core), ep: 8 (over y).
Axes of the slice: x: 4, y: 8, z: 8, core: 2. Of those that a mesh axis runs over, the one named last changes fastest.
Arguments:
- trainer_rows: bfloat16 [8, 8, 7680, 1024], P('ep', None, 'fsdp'), may hold values from -0.0625 to 0.0625
- row_counts: int32 [8, 8, 64], replicated, may hold values from 1 to 120, 7168 in all within a row
- rollout_map: int32 [8, 8], replicated, may hold values from 0 to 7, as said below
Outputs:
- codes: bfloat16 [8, 64, 7168, 128], P('ep', 'fsdp')
- block_scales: float32 [8, 64, 56], P('ep', 'fsdp')
Inputs may be any that keep to these rules, and one draw needn't show every extreme that they name: For each k the entries rollout_map[k, g] over g are a permutation of the rollout devices; each trainer group sends exactly 1 of its experts to each rollout device. `row_counts`: the counts of one expert over the shards sum to 7168; in every expert some shard holds 120 rows.
All inputs are finite; a program needn't handle non-finite values. Where the computation divides by a largest or mean magnitude, that divisor is 1e-20 or more.
Results may differ from a plain program's by a relative error of at most 0.001.
Values may be sent and summed in bfloat16 or wider, within the bound.
A program may use at most 64 MiB of HBM per device.

v0:
```python
import jax
import jax.numpy as jnp
from jax import lax
from jax.sharding import PartitionSpec as P

H = 7168
BLOCK = 128


EPSILON = 1e-06
CODE_RANGE = 448.0


def order_ranks(rollout_map):
    per_group = rollout_map.shape[0]
    position = jnp.arange(per_group, dtype=jnp.int32)
    earlier = position[:, None] < position[None, :]
    same = rollout_map[:, None, :] == rollout_map[None, :, :]
    return jnp.sum((same & earlier[:, :, None]).astype(jnp.int32), axis=0)


def compact_rows(buffer, counts, buffer_rows):
    total_rows, width = buffer.shape
    block_count = H // BLOCK
    spare = total_rows - H
    extra_blocks = (spare + BLOCK - 1) // BLOCK
    blocked = buffer.reshape(block_count + extra_blocks, BLOCK, width)
    windows = jnp.concatenate(
        [blocked[shift : shift + block_count] for shift in range(extra_blocks + 1)], axis=1
    )
    ends = jnp.cumsum(counts)
    height = jnp.arange(H, dtype=jnp.int32)
    passed = (ends[None, :] <= height[:, None]).astype(jnp.int32)
    offset = jnp.sum(passed * (buffer_rows - counts)[None, :], axis=1)
    within = (height % BLOCK + offset).reshape(block_count, BLOCK)
    window_pos = jnp.arange((extra_blocks + 1) * BLOCK, dtype=jnp.int32)
    picker = (within[:, :, None] == window_pos[None, None, :]).astype(jnp.bfloat16)
    picked = jnp.einsum("bpw,bwc->bpc", picker, windows, preferred_element_type=jnp.float32)
    return picked.astype(jnp.bfloat16).reshape(H, width)


def quantize(slab):
    values = slab.astype(jnp.float32).reshape(H // BLOCK, BLOCK, BLOCK)
    denom = jnp.max(jnp.abs(values), axis=(1, 2)) + EPSILON
    codes = (values / denom[:, None, None]).reshape(H, BLOCK).astype(jnp.bfloat16)
    return (codes, denom / CODE_RANGE)


def on_device(trainer_rows, row_counts, rollout_map):
    local = trainer_rows[0]
    per_group, buffer_rows, columns = local.shape
    ep_count = lax.axis_size("ep")
    fsdp_count = lax.axis_size("fsdp")
    per_pair = per_group // ep_count
    col_blocks = columns // BLOCK
    slab_count = per_group * col_blocks // fsdp_count
    group = lax.axis_index("ep")
    fsdp_at = lax.axis_index("fsdp")
    ranks = order_ranks(rollout_map)
    position = jnp.arange(per_group, dtype=jnp.int32)
    tiles = local.reshape(per_group, buffer_rows, col_blocks, BLOCK)
    targets = lax.dynamic_index_in_dim(rollout_map, group, 1, keepdims=False)
    own_ranks = lax.dynamic_index_in_dim(ranks, group, 1, keepdims=False)
    select = targets[None, None, :] == jnp.arange(ep_count, dtype=jnp.int32)[:, None, None]
    select = select & (
        own_ranks[None, None, :] == jnp.arange(per_pair, dtype=jnp.int32)[None, :, None]
    )
    placed = jnp.einsum(
        "jpk,krcl->jpcrl", select.astype(jnp.bfloat16), tiles, preferred_element_type=jnp.float32
    )
    outgoing = placed.astype(jnp.bfloat16).reshape(per_group * col_blocks, buffer_rows, BLOCK)
    owned = lax.all_to_all(outgoing, "ep", split_axis=0, concat_axis=0, tiled=True)
    arrived = lax.all_to_all(owned, "fsdp", split_axis=0, concat_axis=1, tiled=True)

    def settle(slab_at, buffer):
        slot_id = (fsdp_at * slab_count + slab_at) // col_blocks
        source = slot_id // per_pair
        within = slot_id % per_pair
        hit = (rollout_map[:, source] == group) & (ranks[:, source] == within)
        expert_at = jnp.sum(jnp.where(hit, position, 0))
        counts = row_counts[source, expert_at]
        return compact_rows(buffer, counts, buffer_rows)

    slabs = jax.vmap(settle)(jnp.arange(slab_count, dtype=jnp.int32), arrived)
    codes, scales = jax.vmap(quantize)(slabs)
    return (codes[None], scales[None])


def solution(mesh):
    placed = (P("ep", None, "fsdp", None), P(), P())
    return jax.shard_map(
        on_device,
        mesh=mesh,
        in_specs=placed,
        out_specs=(P("ep", "fsdp", None, None), P("ep", "fsdp", None)),
        check_vma=False,
    )
```

profile of v0, /device:TPU:1, one launch (start us, length us, event | category | flops | bytes accessed | tf_op | source)
XLA Modules:
  0.0 135.5 jit_solution(14292810483558981429)
XLA Ops:
  0.6 0.0 copy-start
  0.7 0.8 convert_reduce_fusion
  1.5 0.9 dynamic-slice_reduce_fusion
  2.4 2.1 %copy.13 = bf16[120,8,8,128]{3,2,1,0:T(8,128)(2,1)S(1)} copy(bf16[120,8,8,128]{3,1,2,0:T(8,128)(2,1)} %bitcast.55) | data formatting | bytes 3932160
  4.5 0.0 copy-done
  4.5 0.2 fusion.16
  4.7 1.2 convert_bitcast_fusion
  6.0 1.3 copy.11
  7.2 53.0 %all_to_all.14 = bf16[64,120,128]{2,1,0:T(8,128)(2,1)} all-to-all(bf16[64,120,128]{2,1,0:T(8,128)(2,1)S(1)} %bitcast.53), channel_id=1, replica_groups=mesh['fsdp'=64,'ep'=8] {'ep'}, dimensions={0} | all-to-all | bytes 3932160 | tf_op jit(solution)/shard_map/all_to_all | solution.py:72
  60.2 17.2 %all-to-all-start.1 = ((bf16[64,120,128]{2,1,0:T(8,128)(2,1)}), bf16[64,120,128]{2,1,0:T(8,128)(2,1)S(1)}, u32[]{:S(2)}, u32[]{:S(2)}) async-start(bf16[64,120,128]{2,1,0:T(8,128)(2,1)} %all_to_all.14), calls=%async_computation.1 | async-start | bytes 3932160 | tf_op jit(solution)/shard_map/all_to_all | solution.py:73
  77.5 0.6 fusion.19
  80.0 0.7 fusion.20
  80.8 0.2 reduce_window_sum.14
  81.0 0.3 select_reduce_fusion
  81.3 43.1 %all-to-all-done.1 = bf16[64,120,128]{2,1,0:T(8,128)(2,1)S(1)} async-done(((bf16[64,120,128]{2,1,0:T(8,128)(2,1)}), bf16[64,120,128]{2,1,0:T(8,128)(2,1)S(1)}, u32[]{:S(2)}, u32[]{:S(2)}) %all-to-all-start.1) | async-done | bytes 1966112 | tf_op jit(solution)/shard_map/all_to_all | solution.py:73
  124.4 0.1 slice_dynamic-update-slice_fusion.4
  124.5 0.2 slice_dynamic-update-slice_fusion.3
  124.8 0.2 slice_dynamic-update-slice_fusion.2
  125.0 0.2 slice_dynamic-update-slice_fusion.1
  125.3 0.2 slice_dynamic-update-slice_fusion
  125.5 5.4 %abs_reduce_fusion = (f32[56]{0:T(128)S(1)}, f32[56,128,128]{2,1,0:T(8,128)S(1)}) fusion(bf16[1,56,640,128]{3,2,1,0:T(8,128)(2,1)S(1)} %slice_dynamic-update-slice_fusion, s32[56,128]{1,0:T(8,128)S(1)} %fusion.10), kind=kOutput, calls=%fused_computation.5 | convolution fusion | flops 1182662656 | bytes 12873952 | tf_op jit(solution)/shard_map/vmap(bpw,bwc->bpc)/dot_general | solution.py:38
  131.0 0.5 multiply_bitcast_fusion
  131.5 0.1 broadcast_bitcast_fusion
  131.6 3.9 %divide_convert_fusion = bf16[1,1,7168,128]{3,2,1,0:T(8,128)(2,1)} fusion(f32[1,1,7168,128]{3,2,1,0:T(8,128)S(1)} %bitcast.54, f32[7168]{0:T(1024)S(1)} %broadcast_bitcast_fusion), kind=kLoop, calls=%fused_computation.4 | loop fusion | flops 1835008 | bytes 5533696 | tf_op jit(solution)/shard_map/vmap()/convert_element_type | solution.py:45
  (2 shorter events, 0.0 us)
Async XLA Ops:
  0.6 3.9 %copy-start = (s32[8,8]{1,0:T(8,128)S(1)}, s32[8,8]{1,0:T(8,128)}, u32[]{:S(2)}) copy-start(s32[8,8]{1,0:T(8,128)} %param.5) | copy-start | bytes 772
  60.2 64.2 %all-to-all-start.1 = ((bf16[64,120,128]{2,1,0:T(8,128)(2,1)}), bf16[64,120,128]{2,1,0:T(8,128)(2,1)S(1)}, u32[]{:S(2)}, u32[]{:S(2)}) async-start(bf16[64,120,128]{2,1,0:T(8,128)(2,1)} %all_to_all.14), calls=%async_computation.1 | async-start | bytes 3932160 | tf_op jit(solution)/shard_map/all_to_all | solution.py:73
where the time goes:
time: 136 us; the launch traced here: 135 us
  blocking collectives  53 us (39%)
  waiting for transfers between devices  43.1 us (32%)
  starting transfers between devices  17.2 us (13%)
  other arithmetic  7.36 us (5%)
  matrix products  6.68 us (5%)
  local copies, waits for them, and re-layouts  5.41 us (4%)
  between operations  2.72 us (2%)
    all_to_all x1, blocking collectives, on_device(): lax.all_to_all(outgoing, 'ep', split_axis=0, concat_axis=0, tiled=True)  53 us
    all_to_all x1, waiting for transfers between devices, on_device(): lax.all_to_all(owned, 'fsdp', split_axis=0, concat_axis=1, tiled=True)  43.1 us
    all_to_all x1, starting transfers between devices, on_device(): lax.all_to_all(owned, 'fsdp', split_axis=0, concat_axis=1, tiled=True)  17.2 us
    dot_general x1, matrix products, compact_rows(): jnp.einsum('bpw,bwc->bpc', picker, windows, preferred_element_type=jnp.fl...  5.45 us
    convert_element_type x1, other arithmetic, quantize(): (values / denom[:, None, None]).reshape(H, BLOCK).astype(jnp.bfloat16)  3.91 us
    unnamed x7, local copies, waits for them, and re-layouts  2.96 us
  transfers between devices with their start and end apart: 1, of which 1 were waited for; matrix products, arithmetic and copies ran while one was open for 1% of the time, Pallas kernels for 0%

commit v1 on v0

v1 whole, which is shorter than its diff:
```python
import functools

import jax
import jax.numpy as jnp
from jax import lax
from jax.experimental import pallas as pl
from jax.experimental.pallas import tpu as pltpu
from jax.sharding import PartitionSpec as P

BLOCK = 128
EPSILON = 1e-06
CODE_RANGE = 448.0
LAG = 2
MESH = pl.DeviceIdType.MESH


def chunk_order(nx):
    order = [0, 2, 1, 3] if nx == 4 else list(range(nx))
    return [(dx, 0) for dx in order] + [(dx, 1) for dx in order[1:] + order[:1]]


def exchange_kernel(ny, nx, lag, map_ref, counts_ref, rows_ref, out_ref, send, relay, shift, ssem, s2sem, rsem, fsem):
    nxc = 2 * nx
    order = chunk_order(nx)
    cap = rows_ref.shape[1]
    f = lax.axis_index("fsdp")
    y = lax.axis_index("ep")
    z, xc = f // nxc, f % nxc
    x, core = xc // 2, xc % 2
    home = z == y

    barrier = pltpu.get_barrier_semaphore()

    def greet_plane(n, carry):
        to_xc, to_y = n // ny, n % ny

        @pl.when(jnp.logical_not((to_xc == xc) & (to_y == y)))
        def _():
            pl.semaphore_signal(barrier, inc=1, device_id=(z * nxc + to_xc, to_y), device_id_type=MESH)

        return carry

    def greet_column(n, carry):
        @pl.when(n != z)
        def _():
            pl.semaphore_signal(barrier, inc=1, device_id=(n * nxc + xc, y), device_id_type=MESH)

        return carry

    lax.fori_loop(0, nxc * ny, greet_plane, 0)
    lax.fori_loop(0, ny, greet_column, 0)

    mine = counts_ref[y].astype(jnp.float32)
    before = lax.broadcasted_iota(jnp.int32, mine.shape, 1) < f
    start = jnp.sum(jnp.where(before, mine, 0.0), axis=1, keepdims=True)
    start = start - cap * jnp.floor((start + 0.5) * (1.0 / cap))
    shift[...] = jnp.broadcast_to(start, shift.shape)
    gap = (
        lax.broadcasted_iota(jnp.int32, (cap, cap), 0) - lax.broadcasted_iota(jnp.int32, (cap, cap), 1)
    ).astype(jnp.float32)

    def offset(i):
        back = ny - 1 - i
        return ((back + 1) // 2) * (1 - 2 * ((back + 1) % 2)) + ny

    def tile(q, i):
        dx, dc = order[q]
        to_xc = ((x + (1 - 2 * core) * dx + nx) % nx) * 2 + (core + dc) % 2
        to_y = (y + offset(i)) % ny
        expert = 0
        for k in range(rows_ref.shape[0]):
            expert = jnp.where(map_ref[k, y] == to_y, k, expert)
        turn = shift[pl.ds(expert, 1), :][:, :cap]
        picker = ((gap == turn) | (gap == turn - cap)).astype(jnp.bfloat16)
        rows = rows_ref[expert, :, pl.ds(pl.multiple_of(to_xc * BLOCK, BLOCK), BLOCK)]
        turned = jnp.dot(picker, rows, preferred_element_type=jnp.float32)
        send[q * ny + i] = turned.astype(jnp.bfloat16)
        return to_xc, to_y

    def first_leg(q, i, to_xc, to_y):
        slot = q * ny + i
        own = (to_y == y) & (to_xc == xc)
        source = send.at[slot]

        @pl.when(jnp.logical_not(own) & jnp.logical_not(home))
        def _():
            pltpu.make_async_remote_copy(
                src_ref=source, dst_ref=relay.at[slot], send_sem=ssem, recv_sem=rsem.at[slot],
                device_id=(z * nxc + to_xc, to_y), device_id_type=MESH,
            ).start()

        @pl.when(jnp.logical_not(own) & home)
        def _():
            pltpu.make_async_remote_copy(
                src_ref=source, dst_ref=out_ref.at[f], send_sem=ssem, recv_sem=fsem,
                device_id=(z * nxc + to_xc, to_y), device_id_type=MESH,
            ).start()

        if order[q] == (0, 0):

            @pl.when(own & jnp.logical_not(home))
            def _():
                pltpu.make_async_remote_copy(
                    src_ref=source, dst_ref=out_ref.at[f], send_sem=ssem, recv_sem=fsem,
                    device_id=(y * nxc + xc, y), device_id_type=MESH,
                ).start()

            @pl.when(own & home)
            def _():
                pltpu.make_async_copy(source, out_ref.at[f], fsem).start()

    def second_leg(q, i):
        dx, dc = order[q]
        slot = q * ny + i
        from_y = (y - offset(i) + 2 * ny) % ny
        from_core = (core + dc) % 2
        from_xc = ((x - (1 - 2 * from_core) * dx + nx) % nx) * 2 + from_core
        moves = from_y != z
        if order[q] == (0, 0):
            moves = moves & (from_y != y)

        @pl.when(moves)
        def _():
            pltpu.make_async_copy(relay.at[slot], relay.at[slot], rsem.at[slot]).wait()
            pltpu.make_async_remote_copy(
                src_ref=relay.at[slot], dst_ref=out_ref.at[z * nxc + from_xc], send_sem=s2sem, recv_sem=fsem,
                device_id=(from_y * nxc + xc, y), device_id_type=MESH,
            ).start()

    chunks = len(order)
    for q in range(chunks + lag):
        if q < chunks:

            def push(i, carry):
                to_xc, to_y = tile(q, i)
                if q == 0:

                    @pl.when(i == 0)
                    def _():
                        pl.semaphore_wait(barrier, nxc * ny - 1 + ny - 1)

                first_leg(q, i, to_xc, to_y)
                return carry

            lax.fori_loop(0, ny, push, 0)
        if q >= lag:

            def pass_on(i, carry):
                second_leg(q - lag, i)
                return carry

            lax.fori_loop(0, ny, pass_on, 0)

    pltpu.make_async_copy(out_ref, out_ref, fsem).wait()
    total = nxc * ny

    @pl.when(home)
    def _():
        sent = send.at[pl.ds(0, total - 1)]
        pltpu.make_async_copy(sent, sent, ssem).wait()
        passed = relay.at[pl.ds(0, total - nxc)]
        pltpu.make_async_copy(passed, passed, s2sem).wait()

    @pl.when(jnp.logical_not(home))
    def _():
        pltpu.make_async_copy(send, send, ssem).wait()
        passed = relay.at[pl.ds(0, total - nxc - 1)]
        pltpu.make_async_copy(passed, passed, s2sem).wait()


def exchange(rows, row_counts, rollout_map, ny, nz, nx, lag=LAG, cid=0, name="exchange"):
    experts, cap, width = rows.shape
    tiles = (2 * nx * ny, cap, BLOCK)
    return pl.pallas_call(
        functools.partial(exchange_kernel, ny, nx, lag),
        name=name,
        out_shape=jax.ShapeDtypeStruct(tiles, jnp.bfloat16),
        in_specs=[
            pl.BlockSpec(memory_space=pltpu.SMEM),
            pl.BlockSpec(memory_space=pltpu.VMEM),
            pl.BlockSpec(memory_space=pltpu.VMEM),
        ],
        out_specs=pl.BlockSpec(memory_space=pl.ANY),
        scratch_shapes=[
            pltpu.VMEM(tiles, jnp.bfloat16),
            pltpu.VMEM(tiles, jnp.bfloat16),
            pltpu.VMEM((experts, 128), jnp.float32),
            pltpu.SemaphoreType.DMA,
            pltpu.SemaphoreType.DMA,
            pltpu.SemaphoreType.DMA((tiles[0],)),
            pltpu.SemaphoreType.DMA,
        ],
        compiler_params=pltpu.CompilerParams(
            collective_id=cid, has_side_effects=True, vmem_limit_bytes=32 << 20
        ),
    )(rollout_map, row_counts, rows)


def settle_kernel(
    nxc, parts, map_ref, counts_ref, tiles_ref, codes_ref, scales_ref, held, flat, most, codes, in_sem, out_sem
):
    shards, cap, _ = tiles_ref.shape
    blocks = most.shape[0]
    f = lax.axis_index("fsdp")
    y = lax.axis_index("ep")
    group = f // nxc
    expert = 0
    for k in range(map_ref.shape[0]):
        expert = jnp.where(map_ref[k, group] == y, k, expert)

    step = shards // parts

    def fetch(p):
        rows = pl.ds(p * step, step)
        return pltpu.make_async_copy(tiles_ref.at[rows], held.at[rows], in_sem.at[p])

    for p in range(parts):
        fetch(p).start()
    row = lax.broadcasted_iota(jnp.int32, (cap, BLOCK), 0)

    def place(n, carry):
        page, start, current = carry
        count = counts_ref[group, expert, n]
        here = held[n].astype(jnp.float32)
        current = jnp.where(row >= start, here, current)
        flat[pl.ds(pl.multiple_of(page * cap, 8), cap), :] = current
        start = start + count
        spill = start >= cap
        current = jnp.where(spill, here, current)
        return page + jnp.where(spill, 1, 0), start - jnp.where(spill, cap, 0), current

    carry = (jnp.int32(0), jnp.int32(0), jnp.zeros((cap, BLOCK), jnp.float32))
    for p in range(parts):
        fetch(p).wait()
        carry = lax.fori_loop(p * step, (p + 1) * step, place, carry)
    page, _, current = carry
    flat[pl.ds(pl.multiple_of(page * cap, 8), cap), :] = current

    def largest(b, carry):
        block = flat[pl.ds(pl.multiple_of(b * BLOCK, BLOCK), BLOCK), :]
        most[pl.ds(b, 1), :] = jnp.max(jnp.abs(block), axis=0, keepdims=True)
        return carry

    lax.fori_loop(0, blocks, largest, 0, unroll=4)
    denom = jnp.max(most[...], axis=1, keepdims=True) + EPSILON
    wide = jnp.broadcast_to(denom, most.shape)
    at = lax.broadcasted_iota(jnp.int32, wide.shape, 0)
    lane = lax.broadcasted_iota(jnp.int32, wide.shape, 1)
    line = jnp.sum(jnp.where(at == lane, wide, 0.0), axis=0, keepdims=True)
    scales_ref[0] = (line / CODE_RANGE)[:, :blocks]
    most[...] = 1.0 / wide

    def divide(b, carry):
        rows = pl.ds(pl.multiple_of(b * BLOCK, BLOCK), BLOCK)
        codes[rows, :] = (flat[rows, :] * most[pl.ds(b, 1), :]).astype(jnp.bfloat16)
        return carry

    share = blocks // parts

    def deliver(p):
        rows = pl.ds(p * share * BLOCK, share * BLOCK)
        return pltpu.make_async_copy(codes.at[rows], codes_ref.at[0, 0, rows], out_sem.at[p])

    for p in range(parts):
        lax.fori_loop(p * share, (p + 1) * share, divide, 0)
        deliver(p).start()
    for p in range(parts):
        deliver(p).wait()


def settle(tiles, row_counts, rollout_map, nxc, height, parts):
    shards, cap, _ = tiles.shape
    blocks = height // BLOCK
    pages = height // cap + 2
    return pl.pallas_call(
        functools.partial(settle_kernel, nxc, parts),
        name="settle",
        out_shape=(
            jax.ShapeDtypeStruct((1, 1, height, BLOCK), jnp.bfloat16),
            jax.ShapeDtypeStruct((1, 1, blocks), jnp.float32),
        ),
        in_specs=[
            pl.BlockSpec(memory_space=pltpu.SMEM),
            pl.BlockSpec(memory_space=pltpu.SMEM),
            pl.BlockSpec(memory_space=pl.ANY),
        ],
        out_specs=(pl.BlockSpec(memory_space=pl.ANY), pl.BlockSpec(memory_space=pltpu.VMEM)),
        scratch_shapes=[
            pltpu.VMEM(tiles.shape, jnp.bfloat16),
            pltpu.VMEM((pages * cap, BLOCK), jnp.float32),
            pltpu.VMEM((blocks, BLOCK), jnp.float32),
            pltpu.VMEM((height, BLOCK), jnp.bfloat16),
            pltpu.SemaphoreType.DMA((parts,)),
            pltpu.SemaphoreType.DMA((parts,)),
        ],
        compiler_params=pltpu.CompilerParams(vmem_limit_bytes=32 << 20),
    )(rollout_map, row_counts, tiles)


def on_device(height, trainer_rows, row_counts, rollout_map):
    ny = lax.axis_size("ep")
    nxc = trainer_rows.shape[-1] // BLOCK
    nz = lax.axis_size("fsdp") // nxc
    tiles = exchange(trainer_rows[0], row_counts, rollout_map, ny, nz, nxc // 2)
    parts = 8 if height % (8 * BLOCK) == 0 else 1
    return settle(tiles, row_counts, rollout_map, nxc, height, parts)


def solution(mesh, height=7168):
    placed = (P("ep", None, "fsdp", None), P(), P())
    return jax.shard_map(
        functools.partial(on_device, height),
        mesh=mesh,
        in_specs=placed,
        out_specs=(P("ep", "fsdp", None, None), P("ep", "fsdp", None)),
        check_vma=False,
    )
```

time: 136 us -> 83.3 us (0.61)
  Pallas kernels: 0 us -> 79.4 us
  blocking collectives: 53 us -> 0 us
  waiting for transfers between devices: 43.1 us -> 0 us
  starting transfers between devices: 17.2 us -> 0 us
  other arithmetic: 7.36 us -> 0 us
  matrix products: 6.68 us -> 0 us
  local copies, waits for them, and re-layouts: 5.41 us -> 2.98 us
  between operations: 2.72 us -> 0.65 us
    pallas_call x0 -> x2, Pallas kernels: none -> 79.4 us  [the longest x1 72.5 us: exchange(): pl.pallas_call(functools.partial(exchange_kernel, ny, nx, lag), name=name...]
    all_to_all x1 -> x0, blocking collectives: 53 us -> none  [on_device(): lax.all_to_all(outgoing, 'ep', split_axis=0, concat_axis=0, tiled=True)]
    all_to_all x1 -> x0, waiting for transfers between devices: 43.1 us -> none  [on_device(): lax.all_to_all(owned, 'fsdp', split_axis=0, concat_axis=1, tiled=True)]
    all_to_all x1 -> x0, starting transfers between devices: 17.2 us -> none  [on_device(): lax.all_to_all(owned, 'fsdp', split_axis=0, concat_axis=1, tiled=True)]
    dot_general x2 -> x0, matrix products: 6.68 us -> none  [the longest x1 5.45 us: compact_rows(): jnp.einsum('bpw,bwc->bpc', picker, windows, preferred_element_type=jnp.fl...]
    convert_element_type x1 -> x0, other arithmetic: 3.91 us -> none  [quantize(): (values / denom[:, None, None]).reshape(H, BLOCK).astype(jnp.bfloat16)]
    reduce_sum x3 -> x0, other arithmetic: 1.76 us -> none  [the longest x1 0.82 us: order_ranks(): return jnp.sum((same & earlier[:, :, None]).astype(jnp.int32), axis=0)]
    unnamed x7 -> x6, local copies, waits for them, and re-layouts: 2.96 us -> 2.98 us
  transfers between devices with their start and end apart: 1 -> 0, of which waited for: 1 -> 0; matrix products, arithmetic and copies ran while one was open for 1% -> 0% of each run, Pallas kernels for 0% -> 0%
where the time goes in v1:
time: 83.3 us; the launch traced here: 83.1 us
  Pallas kernels  79.4 us (95%)
  local copies, waits for them, and re-layouts  2.98 us (4%)
    pallas_call x1, Pallas kernels, exchange(): pl.pallas_call(functools.partial(exchange_kernel, ny, nx, lag), name=name...  72.5 us
    pallas_call x1, Pallas kernels, settle(): pl.pallas_call(functools.partial(settle_kernel, nxc, parts), name='settle...  6.93 us
    unnamed x6, local copies, waits for them, and re-layouts  2.98 us

profile of v1, /device:TPU:1, one launch (start us, length us, event | category | flops | bytes accessed | tf_op | source)
XLA Modules:
  0.0 83.1 jit_solution(1349693593315552558)
XLA Ops:
  0.6 0.0 copy-start
  0.6 1.5 %copy-done = bf16[1,8,120,1024]{3,2,1,0:T(8,128)(2,1)S(1)} copy-done((bf16[1,8,120,1024]{3,2,1,0:T(8,128)(2,1)S(1)}, bf16[1,8,120,1024]{3,2,1,0:T(8,128)(2,1)}, u32[]{:S(2)}) %copy-start) | copy-done | bytes 1966104
  2.2 0.0 copy-start.1
  2.2 0.8 copy-done.1
  2.9 0.0 copy-start.2
  2.9 0.7 copy-done.2
  3.6 72.5 %exchange.1.tiles_ref = bf16[64,120,128]{2,1,0:T(8,128)(2,1)S(1)} custom-call(s32[8,8]{1,0:T(8,128)S(1)} %copy-done.2, s32[8,8,64]{2,1,0:T(8,128)S(1)} %copy-done.1, bf16[8,120,1024]{2,1,0:T(8,128)(2,1)S(1)} %bitcast.1), custom_call_target="tpu_custom_call" | custom-call | tf_op jit(solution)/shard_map/exchange/pallas_call | solution.py:174
  76.1 6.9 %settle.1 = (bf16[1,1,7168,128]{3,2,1,0:T(8,128)(2,1)}, f32[1,1,56]{2,1,0:T(1,128)}) custom-call(s32[8,8]{1,0:T(8,128)S(1)} %copy-done.2, s32[8,8,64]{2,1,0:T(8,128)S(1)} %copy-done.1, bf16[64,120,128]{2,1,0:T(8,128)(2,1)S(1)} %exchange.1.tiles_ref), custom_call_target="tpu_custom_call" | custom-call | tf_op jit(solution)/shard_map/settle/pallas_call | solution.py:275
Async XLA Ops:
  0.6 1.5 %copy-start = (bf16[1,8,120,1024]{3,2,1,0:T(8,128)(2,1)S(1)}, bf16[1,8,120,1024]{3,2,1,0:T(8,128)(2,1)}, u32[]{:S(2)}) copy-start(bf16[1,8,120,1024]{3,2,1,0:T(8,128)(2,1)} %param.3) | copy-start | bytes 5898244
  2.2 0.8 copy-start.1
  2.9 0.7 copy-start.2

commit v2 on v1

v2 whole, which is shorter than its diff:
```python
import functools

import jax
import jax.numpy as jnp
from jax import lax
from jax.experimental import pallas as pl
from jax.experimental.pallas import tpu as pltpu
from jax.sharding import PartitionSpec as P

BLOCK = 128
EPSILON = 1e-06
CODE_RANGE = 448.0
LAG = 2
REST = 2
MESH = pl.DeviceIdType.MESH


def chunk_order(nx):
    order = [0, 2, 1, 3] if nx == 4 else list(range(nx))
    return [(dx, 0) for dx in order] + [(dx, 1) for dx in order[1:] + order[:1]]


def exchange_kernel(
    ny, nx, back, lag, rest, map_hbm, counts_hbm, rows_hbm, flat,
    map_ref, counts_ref, rows_ref, send, relay, held, shift, bounds, picker, in_sem, ssem, s2sem, rsem, fsem,
):
    nxc = 2 * nx
    order = chunk_order(nx)
    chunks = len(order)
    experts, cap, _ = rows_ref.shape
    f = lax.axis_index("fsdp")
    y = lax.axis_index("ep")
    z, xc = f // nxc, f % nxc
    x, core = xc // 2, xc % 2
    home = z == y

    fetches = [
        pltpu.make_async_copy(source, target, in_sem.at[n])
        for n, (source, target) in enumerate(
            ((map_hbm, map_ref), (counts_hbm, counts_ref), (rows_hbm.at[0], rows_ref))
        )
    ]
    for fetch in fetches:
        fetch.start()

    barrier = pltpu.get_barrier_semaphore()

    def greet_plane(n, carry):
        to_xc, to_y = n // ny, n % ny

        @pl.when(jnp.logical_not((to_xc == xc) & (to_y == y)))
        def _():
            pl.semaphore_signal(barrier, inc=1, device_id=(z * nxc + to_xc, to_y), device_id_type=MESH)

        return carry

    def greet_column(n, carry):
        @pl.when(n != z)
        def _():
            pl.semaphore_signal(barrier, inc=1, device_id=(n * nxc + xc, y), device_id_type=MESH)

        return carry

    lax.fori_loop(0, nxc * ny, greet_plane, 0)
    lax.fori_loop(0, ny, greet_column, 0)

    def offset(i):
        return ((i + 1) // 2) * (1 - 2 * ((i + 1) % 2)) + ny

    fetches[0].wait()
    fetches[1].wait()
    mine = counts_ref[y].astype(jnp.float32)
    before = lax.broadcasted_iota(jnp.int32, mine.shape, 1) < f
    start = jnp.sum(jnp.where(before, mine, 0.0), axis=1, keepdims=True)
    start = start - cap * jnp.floor((start + 0.5) * (1.0 / cap))
    shift[...] = jnp.broadcast_to(start, shift.shape)
    gap = (
        lax.broadcasted_iota(jnp.int32, (cap, cap), 0) - lax.broadcasted_iota(jnp.int32, (cap, cap), 1)
    ).astype(jnp.float32)
    chosen = []
    for i in range(ny):
        expert = 0
        for k in range(experts):
            expert = jnp.where(map_ref[k, y] == (y + offset(i)) % ny, k, expert)
        chosen.append(expert)
        turn = shift[pl.ds(expert, 1), :][:, :cap]
        picker[i] = ((gap == turn) | (gap == turn - cap)).astype(jnp.bfloat16)
    fetches[2].wait()

    def column(q):
        dx, dc = order[q]
        return ((x + (1 - 2 * core) * dx + nx) % nx) * 2 + (core + dc) % 2

    def source_column(q):
        dx, dc = order[q]
        from_core = (core + dc) % 2
        return ((x - (1 - 2 * from_core) * dx + nx) % nx) * 2 + from_core

    def turn_rows(q):
        lanes = pl.ds(pl.multiple_of(column(q) * BLOCK, BLOCK), BLOCK)
        for i in range(ny):
            turned = jnp.dot(picker[i], rows_ref[chosen[i], :, lanes], preferred_element_type=jnp.float32)
            send[q * ny + i] = turned.astype(jnp.bfloat16)

    def first_leg(q, i):
        slot = q * ny + i
        to_xc, to_y = column(q), (y + offset(i)) % ny
        own = (to_y == y) & (to_xc == xc)
        source = send.at[slot]
        landing = held.at[q * ny + z]

        @pl.when(jnp.logical_not(own) & jnp.logical_not(home))
        def _():
            pltpu.make_async_remote_copy(
                src_ref=source, dst_ref=relay.at[slot], send_sem=ssem, recv_sem=rsem.at[slot],
                device_id=(z * nxc + to_xc, to_y), device_id_type=MESH,
            ).start()

        @pl.when(jnp.logical_not(own) & home)
        def _():
            pltpu.make_async_remote_copy(
                src_ref=source, dst_ref=landing, send_sem=ssem, recv_sem=fsem.at[q],
                device_id=(z * nxc + to_xc, to_y), device_id_type=MESH,
            ).start()

        if order[q] == (0, 0):

            @pl.when(own & jnp.logical_not(home))
            def _():
                pltpu.make_async_remote_copy(
                    src_ref=source, dst_ref=landing, send_sem=ssem, recv_sem=fsem.at[q],
                    device_id=(y * nxc + xc, y), device_id_type=MESH,
                ).start()

            @pl.when(own & home)
            def _():
                pltpu.make_async_copy(source, landing, fsem.at[q]).start()

    def second_leg(q, i):
        slot = q * ny + i
        from_y = (y - offset(i) + 2 * ny) % ny
        moves = from_y != z
        if order[q] == (0, 0):
            moves = moves & (from_y != y)

        @pl.when(moves)
        def _():
            pltpu.make_async_copy(relay.at[slot], relay.at[slot], rsem.at[slot]).wait()
            pltpu.make_async_remote_copy(
                src_ref=relay.at[slot], dst_ref=held.at[q * ny + z], send_sem=s2sem, recv_sem=fsem.at[q],
                device_id=(from_y * nxc + xc, y), device_id_type=MESH,
            ).start()

    row = lax.broadcasted_iota(jnp.int32, (cap, BLOCK), 0).astype(jnp.float32)

    def find_bounds():
        expert = 0
        for k in range(experts):
            expert = jnp.where(map_ref[k, z] == y, k, expert)
        shards = counts_ref.shape[2]
        counts = jnp.broadcast_to(counts_ref[z, pl.ds(expert, 1), :].astype(jnp.float32), (shards, shards))
        at = lax.broadcasted_iota(jnp.int32, counts.shape, 0)
        other = lax.broadcasted_iota(jnp.int32, counts.shape, 1)
        for n, kept in enumerate((other < at, other <= at)):
            ends = jnp.sum(jnp.where(kept, counts, 0.0), axis=1, keepdims=True)
            bounds[n] = jnp.broadcast_to(ends, bounds.shape[1:])

    def place(q, from_z):
        shard = from_z * nxc + source_column(q)
        here = held[q * ny + from_z].astype(jnp.float32)
        base = (shard * cap).astype(jnp.float32)
        first = bounds[0, pl.ds(shard, 1), :] - base
        last = bounds[1, pl.ds(shard, 1), :] - base
        for d in range(back + 1):
            rows = pl.ds(pl.multiple_of((shard + back - d) * cap, 8), cap)
            inside = (row >= first + d * cap) & (row < last + d * cap)
            flat[rows, :] = jnp.where(inside, here, flat[rows, :])

    for q in range(chunks + lag + rest):
        if q < chunks:
            turn_rows(q)
            if q == 0:
                pl.semaphore_wait(barrier, nxc * ny - 1 + ny - 1)

            def push(i, carry):
                first_leg(q, i)
                return carry

            lax.fori_loop(0, ny, push, 0)
        if q == 0:
            find_bounds()
        if lag <= q < chunks + lag:

            def pass_on(i, carry):
                second_leg(q - lag, i)
                return carry

            lax.fori_loop(0, ny, pass_on, 0)
        if q >= lag + rest:
            done = q - lag - rest
            landed = held.at[pl.ds(done * ny, ny)]
            pltpu.make_async_copy(landed, landed, fsem.at[done]).wait()

            def place_one(from_z, carry):
                place(done, from_z)
                return carry

            lax.fori_loop(0, ny, place_one, 0)

    total = nxc * ny

    @pl.when(home)
    def _():
        sent = send.at[pl.ds(0, total - 1)]
        pltpu.make_async_copy(sent, sent, ssem).wait()
        passed = relay.at[pl.ds(0, total - nxc)]
        pltpu.make_async_copy(passed, passed, s2sem).wait()

    @pl.when(jnp.logical_not(home))
    def _():
        pltpu.make_async_copy(send, send, ssem).wait()
        passed = relay.at[pl.ds(0, total - nxc - 1)]
        pltpu.make_async_copy(passed, passed, s2sem).wait()


def pages_back(shards, cap, height):
    return -(-(shards * cap - height) // cap)


def exchange(rows, row_counts, rollout_map, height, ny, nx, lag=LAG, rest=REST, cid=0, name="exchange"):
    _, experts, cap, width = rows.shape
    shards = row_counts.shape[2]
    total = 2 * nx * ny
    back = pages_back(shards, cap, height)
    tiles = pltpu.VMEM((total, cap, BLOCK), jnp.bfloat16)
    return pl.pallas_call(
        functools.partial(exchange_kernel, ny, nx, back, lag, rest),
        name=name,
        out_shape=jax.ShapeDtypeStruct(((shards + back) * cap, BLOCK), jnp.float32),
        in_specs=[pl.BlockSpec(memory_space=pltpu.HBM)] * 3,
        out_specs=pl.BlockSpec(memory_space=pltpu.VMEM),
        scratch_shapes=[
            pltpu.SMEM(rollout_map.shape, jnp.int32),
            pltpu.VMEM(row_counts.shape, jnp.int32),
            pltpu.VMEM(rows.shape[1:], jnp.bfloat16),
            tiles,
            tiles,
            tiles,
            pltpu.VMEM((experts, BLOCK), jnp.float32),
            pltpu.VMEM((2, shards, BLOCK), jnp.float32),
            pltpu.VMEM((ny, cap, cap), jnp.bfloat16),
            pltpu.SemaphoreType.DMA((3,)),
            pltpu.SemaphoreType.DMA,
            pltpu.SemaphoreType.DMA,
            pltpu.SemaphoreType.DMA((total,)),
            pltpu.SemaphoreType.DMA((2 * nx,)),
        ],
        compiler_params=pltpu.CompilerParams(
            collective_id=cid, has_side_effects=True, vmem_limit_bytes=32 << 20
        ),
    )(*[pltpu.with_memory_space_constraint(array, pltpu.HBM) for array in (rollout_map, row_counts, rows)])


def settle_kernel(skip, parts, flat, codes_ref, scales_ref, most, codes, out_sem):
    blocks = most.shape[0]

    def rows_of(b):
        return flat[pl.ds(pl.multiple_of(skip + b * BLOCK, 8), BLOCK), :]

    share = blocks // parts

    def largest(b, carry):
        most[pl.ds(b, 1), :] = jnp.max(jnp.abs(rows_of(b)), axis=0, keepdims=True)
        return carry

    lax.fori_loop(0, blocks, largest, 0, unroll=share)
    denom = jnp.max(most[...], axis=1, keepdims=True) + EPSILON
    wide = jnp.broadcast_to(denom, most.shape)
    at = lax.broadcasted_iota(jnp.int32, wide.shape, 0)
    lane = lax.broadcasted_iota(jnp.int32, wide.shape, 1)
    line = jnp.sum(jnp.where(at == lane, wide, 0.0), axis=0, keepdims=True)
    scales_ref[0] = (line / CODE_RANGE)[:, :blocks]
    most[...] = 1.0 / wide

    def divide(b, carry):
        rows = pl.ds(pl.multiple_of(b * BLOCK, BLOCK), BLOCK)
        codes[rows, :] = (rows_of(b) * most[pl.ds(b, 1), :]).astype(jnp.bfloat16)
        return carry

    def deliver(p):
        rows = pl.ds(p * share * BLOCK, share * BLOCK)
        return pltpu.make_async_copy(codes.at[rows], codes_ref.at[0, 0, rows], out_sem.at[p])

    for p in range(parts):
        lax.fori_loop(p * share, (p + 1) * share, divide, 0, unroll=share)
        deliver(p).start()
    for p in range(parts):
        deliver(p).wait()


def settle(flat, skip, height, name="settle"):
    blocks = height // BLOCK
    parts = 8 if blocks % 8 == 0 else 1
    return pl.pallas_call(
        functools.partial(settle_kernel, skip, parts),
        name=name,
        out_shape=(
            jax.ShapeDtypeStruct((1, 1, height, BLOCK), jnp.bfloat16),
            jax.ShapeDtypeStruct((1, 1, blocks), jnp.float32),
        ),
        in_specs=[pl.BlockSpec(memory_space=pltpu.VMEM)],
        out_specs=(pl.BlockSpec(memory_space=pltpu.HBM), pl.BlockSpec(memory_space=pltpu.VMEM)),
        scratch_shapes=[
            pltpu.VMEM((blocks, BLOCK), jnp.float32),
            pltpu.VMEM((height, BLOCK), jnp.bfloat16),
            pltpu.SemaphoreType.DMA((parts,)),
        ],
        compiler_params=pltpu.CompilerParams(vmem_limit_bytes=32 << 20),
    )(flat)


def on_device(height, trainer_rows, row_counts, rollout_map):
    cap = trainer_rows.shape[2]
    ny = lax.axis_size("ep")
    nx = trainer_rows.shape[3] // BLOCK // 2
    flat = exchange(trainer_rows, row_counts, rollout_map, height, ny, nx)
    return settle(flat, pages_back(row_counts.shape[2], cap, height) * cap, height)


def solution(mesh, height=7168):
    placed = (P("ep", None, "fsdp", None), P(), P())
    return jax.shard_map(
        functools.partial(on_device, height),
        mesh=mesh,
        in_specs=placed,
        out_specs=(P("ep", "fsdp", None, None), P("ep", "fsdp", None)),
        check_vma=False,
    )
```

time: 83.3 us -> 70.3 us (0.84)
  Pallas kernels: 79.4 us -> 68.8 us
  local copies, waits for them, and re-layouts: 2.98 us -> 0 us
    pallas_call x2, Pallas kernels: 79.4 us -> 68.8 us  [the longest x1 66.6 us: exchange(): pl.pallas_call(functools.partial(exchange_kernel, ny, nx, back, lag, rest...]
    unnamed x6 -> x0, local copies, waits for them, and re-layouts: 2.98 us -> none
where the time goes in v2:
time: 70.3 us; the launch traced here: 69.4 us
  Pallas kernels  68.8 us (98%)
    pallas_call x1, Pallas kernels, exchange(): pl.pallas_call(functools.partial(exchange_kernel, ny, nx, back, lag, rest...  66.6 us
    pallas_call x1, Pallas kernels, settle(): pl.pallas_call(functools.partial(settle_kernel, skip, parts), name=name,...  2.16 us

profile of v2, /device:TPU:1, one launch (start us, length us, event | category | flops | bytes accessed | tf_op | source)
XLA Modules:
  0.0 69.4 jit_solution(16454999736438314500)
XLA Ops:
  0.6 66.6 %exchange.1.flat = f32[8280,128]{1,0:T(8,128)S(1)} custom-call(s32[8,8]{1,0:T(8,128)} %map_hbm.1, s32[8,8,64]{2,1,0:T(8,128)} %counts_hbm.1, bf16[1,8,120,1024]{3,2,1,0:T(8,128)(2,1)} %rows_hbm.1), custom_call_target="tpu_custom_call" | custom-call | tf_op jit(solution)/shard_map/exchange/pallas_call | solution.py:236
  67.3 2.2 %settle.1 = (bf16[1,1,7168,128]{3,2,1,0:T(8,128)(2,1)}, f32[1,1,56]{2,1,0:T(1,128)}) custom-call(f32[8280,128]{1,0:T(8,128)S(1)} %exchange.1.flat), custom_call_target="tpu_custom_call" | custom-call | tf_op jit(solution)/shard_map/settle/pallas_call | solution.py:304

commit v3 on v2

v3 whole, which is shorter than its diff:
```python
import functools

import jax
import jax.numpy as jnp
from jax import lax
from jax.experimental import pallas as pl
from jax.experimental.pallas import tpu as pltpu
from jax.sharding import PartitionSpec as P

BLOCK = 128
EPSILON = 1e-06
CODE_RANGE = 448.0
LAG = 8
REST = 3
AHEAD = 4
MESH = pl.DeviceIdType.MESH


def chunk_order(nx):
    if nx == 4:
        return [(0, 0), (0, 1), (1, 0), (3, 0), (1, 1), (3, 1), (2, 0), (2, 1)]
    return [(0, 0), (0, 1)] + [(dx, dc) for dx in range(1, nx) for dc in (0, 1)]


def exchange_kernel(
    ny, nx, back, lag, rest, ahead, map_hbm, counts_hbm, rows_hbm, flat,
    map_ref, chosen, counts_ref, columns, send, middle, relay, held, shift, bounds, picker,
    in_sem, rows_sem, x_sem, y_sem, z_sem, x_here, y_here, here_sem,
):
    nxc = 2 * nx
    order = chunk_order(nx)
    chunks = len(order)
    experts, cap, _ = columns[0].shape
    f = lax.axis_index("fsdp")
    y = lax.axis_index("ep")
    z, xc = f // nxc, f % nxc
    x, core = xc // 2, xc % 2
    home = z == y

    def column(q):
        dx, dc = order[q]
        return ((x + (1 - 2 * core) * dx + nx) % nx) * 2 + (core + dc) % 2

    def source_column(q):
        dx, dc = order[q]
        from_core = (core + dc) % 2
        return ((x - (1 - 2 * from_core) * dx + nx) % nx) * 2 + from_core

    def fetch_column(q):
        lanes = pl.ds(pl.multiple_of(column(q) * BLOCK, BLOCK), BLOCK)
        return pltpu.make_async_copy(rows_hbm.at[0, :, :, lanes], columns[q], rows_sem.at[q])

    fetch_map = pltpu.make_async_copy(map_hbm, map_ref, in_sem.at[0])
    fetch_counts = pltpu.make_async_copy(counts_hbm, counts_ref, in_sem.at[1])
    fetch_map.start()
    fetch_counts.start()
    for q in range(chunks):
        fetch_column(q).start()

    barrier = pltpu.get_barrier_semaphore()
    for d in range(1, ny):
        pl.semaphore_signal(barrier, inc=1, device_id=(f, (y + d) % ny), device_id_type=MESH)
        pl.semaphore_signal(barrier, inc=1, device_id=((z + d) % ny * nxc + xc, y), device_id_type=MESH)
    for d in range(1, nxc):
        pl.semaphore_signal(barrier, inc=1, device_id=(z * nxc + (xc + d) % nxc, y), device_id_type=MESH)

    def paired(i):
        return ((i + 1) // 2) * (1 - 2 * ((i + 1) % 2)) + ny

    def offset(i):
        return paired(i) % ny

    fetch_map.wait()
    fetch_counts.wait()
    mine = counts_ref[y].astype(jnp.float32)
    before = lax.broadcasted_iota(jnp.int32, mine.shape, 1) < f
    start = jnp.sum(jnp.where(before, mine, 0.0), axis=1, keepdims=True)
    start = start - cap * jnp.floor((start + 0.5) * (1.0 / cap))
    shift[...] = jnp.broadcast_to(start, shift.shape)
    gap = (
        lax.broadcasted_iota(jnp.int32, (cap, cap), 0) - lax.broadcasted_iota(jnp.int32, (cap, cap), 1)
    ).astype(jnp.float32)

    def make_picker(step):
        expert = 0
        for k in range(experts):
            expert = jnp.where(map_ref[k, y] == (y + step) % ny, k, expert)
        chosen[step] = expert
        turn = shift[pl.ds(expert, 1), :][:, :cap]
        picker[step] = ((gap == turn) | (gap == turn - cap)).astype(jnp.bfloat16)

    def turn_rows(q, step):
        turned = jnp.dot(picker[step], columns[q][chosen[step]], preferred_element_type=jnp.float32)
        send[q * ny + step] = turned.astype(jnp.bfloat16)

    def along_x(q):
        tiles = pl.ds(q * ny, ny)
        pltpu.make_async_remote_copy(
            src_ref=send.at[tiles], dst_ref=middle.at[tiles], send_sem=x_sem, recv_sem=x_here.at[q],
            device_id=(z * nxc + column(q), y), device_id_type=MESH,
        ).start()

    def along_y(q, i):
        step = offset(i)
        slot = q * ny + step
        source = middle.at[slot] if q > 0 else send.at[slot]
        landing = held.at[q * ny + z]
        landed = here_sem.at[q * ny + z]
        stays = step == 0

        @pl.when(jnp.logical_not(stays) & jnp.logical_not(home))
        def _():
            pltpu.make_async_remote_copy(
                src_ref=source, dst_ref=relay.at[slot], send_sem=y_sem, recv_sem=y_here.at[slot],
                device_id=(f, (y + step) % ny), device_id_type=MESH,
            ).start()

        @pl.when(jnp.logical_not(stays) & home)
        def _():
            pltpu.make_async_remote_copy(
                src_ref=source, dst_ref=landing, send_sem=y_sem, recv_sem=landed,
                device_id=(f, (y + step) % ny), device_id_type=MESH,
            ).start()

        @pl.when(stays & jnp.logical_not(home))
        def _():
            pltpu.make_async_remote_copy(
                src_ref=source, dst_ref=landing, send_sem=y_sem, recv_sem=landed,
                device_id=(y * nxc + xc, y), device_id_type=MESH,
            ).start()

        @pl.when(stays & home)
        def _():
            pltpu.make_async_copy(source, landing, landed).start()

    def along_z(q, i):
        step = offset(i)
        slot = q * ny + step
        from_y = (y - step + ny) % ny

        @pl.when((from_y != z) & (step != 0))
        def _():
            pltpu.make_async_copy(relay.at[slot], relay.at[slot], y_here.at[slot]).wait()
            pltpu.make_async_remote_copy(
                src_ref=relay.at[slot], dst_ref=held.at[q * ny + z], send_sem=z_sem,
                recv_sem=here_sem.at[q * ny + z], device_id=(from_y * nxc + xc, y), device_id_type=MESH,
            ).start()

    row = lax.broadcasted_iota(jnp.int32, (cap, BLOCK), 0).astype(jnp.float32)

    def find_bounds():
        expert = 0
        for k in range(experts):
            expert = jnp.where(map_ref[k, z] == y, k, expert)
        shards = counts_ref.shape[2]
        counts = jnp.broadcast_to(counts_ref[z, pl.ds(expert, 1), :].astype(jnp.float32), (shards, shards))
        at = lax.broadcasted_iota(jnp.int32, counts.shape, 0)
        other = lax.broadcasted_iota(jnp.int32, counts.shape, 1)
        for n, kept in enumerate((other < at, other <= at)):
            ends = jnp.sum(jnp.where(kept, counts, 0.0), axis=1, keepdims=True)
            bounds[n] = jnp.broadcast_to(ends, bounds.shape[1:])

    def place(q, i):
        from_z = (z + offset(i)) % ny
        slot = q * ny + from_z
        pltpu.make_async_copy(held.at[slot], held.at[slot], here_sem.at[slot]).wait()
        shard = from_z * nxc + source_column(q)
        here = held[slot].astype(jnp.float32)
        base = (shard * cap).astype(jnp.float32)
        first = bounds[0, pl.ds(shard, 1), :] - base
        last = bounds[1, pl.ds(shard, 1), :] - base
        for d in range(back + 1):
            rows = pl.ds(pl.multiple_of((shard + back - d) * cap, 8), cap)
            inside = (row >= first + d * cap) & (row < last + d * cap)
            flat[rows, :] = jnp.where(inside, here, flat[rows, :])

    fetch_column(0).wait()
    for i in range(ny):
        step = offset(i)
        make_picker(step)
        turn_rows(0, step)
        if i == 0:
            pl.semaphore_wait(barrier, 2 * (ny - 1) + nxc - 1)
        along_y(0, i)
    ahead = min(ahead, chunks - 1)
    for q in range(1, ahead + 1):
        fetch_column(q).wait()
        for step in range(ny):
            turn_rows(q, step)
        along_x(q)
    find_bounds()

    half = ny // 2
    for q in range(1, chunks + rest + 1):
        if q < chunks:
            tiles = middle.at[pl.ds(q * ny, ny)]
            pltpu.make_async_copy(tiles, tiles, x_here.at[q]).wait()
        if ahead + q < chunks:
            fetch_column(ahead + q).wait()
        for part in range(2):
            behind = (2 * q + part) * half - lag
            z_at, z_from = behind // ny, behind % ny

            def step_of(n, carry):
                i = part * half + n
                if q < chunks:
                    along_y(q, i)
                if ahead + q < chunks:
                    turn_rows(ahead + q, i)
                if 0 <= q - rest < chunks:
                    place(q - rest, i)
                if 0 <= z_at < chunks:
                    along_z(z_at, z_from + n)
                return carry

            lax.fori_loop(0, half, step_of, 0)
        if ahead + q < chunks:
            along_x(ahead + q)
    def drain(buffer, tiles, semaphore):
        if tiles == 0:
            return
        part = buffer.at[pl.ds(0, tiles)]
        pltpu.make_async_copy(part, part, semaphore).wait()

    drain(send, (chunks - 1) * ny, x_sem)

    @pl.when(home)
    def _():
        drain(send, chunks * (ny - 1), y_sem)
        drain(relay, chunks * (ny - 1), z_sem)

    @pl.when(jnp.logical_not(home))
    def _():
        drain(send, chunks * ny, y_sem)
        drain(relay, chunks * (ny - 2), z_sem)


def pages_back(shards, cap, height):
    return -(-(shards * cap - height) // cap)


def exchange(rows, row_counts, rollout_map, height, ny, nx, lag=LAG, rest=REST, ahead=AHEAD, cid=0, name="exchange"):
    _, experts, cap, width = rows.shape
    shards = row_counts.shape[2]
    total = 2 * nx * ny
    back = pages_back(shards, cap, height)
    tiles = pltpu.VMEM((total, cap, BLOCK), jnp.bfloat16)
    return pl.pallas_call(
        functools.partial(exchange_kernel, ny, nx, back, lag, rest, ahead),
        name=name,
        out_shape=jax.ShapeDtypeStruct(((shards + back) * cap, BLOCK), jnp.float32),
        in_specs=[pl.BlockSpec(memory_space=pltpu.HBM)] * 3,
        out_specs=pl.BlockSpec(memory_space=pltpu.VMEM),
        scratch_shapes=[
            pltpu.SMEM(rollout_map.shape, jnp.int32),
            pltpu.SMEM((ny,), jnp.int32),
            pltpu.VMEM(row_counts.shape, jnp.int32),
            [pltpu.VMEM((experts, cap, BLOCK), jnp.bfloat16)] * (2 * nx),
            tiles,
            tiles,
            tiles,
            tiles,
            pltpu.VMEM((experts, BLOCK), jnp.float32),
            pltpu.VMEM((2, shards, BLOCK), jnp.float32),
            pltpu.VMEM((ny, cap, cap), jnp.bfloat16),
            pltpu.SemaphoreType.DMA((2,)),
            pltpu.SemaphoreType.DMA((2 * nx,)),
            pltpu.SemaphoreType.DMA,
            pltpu.SemaphoreType.DMA,
            pltpu.SemaphoreType.DMA,
            pltpu.SemaphoreType.DMA((2 * nx,)),
            pltpu.SemaphoreType.DMA((total,)),
            pltpu.SemaphoreType.DMA((total,)),
        ],
        compiler_params=pltpu.CompilerParams(
            collective_id=cid, has_side_effects=True, vmem_limit_bytes=32 << 20
        ),
    )(*[pltpu.with_memory_space_constraint(array, pltpu.HBM) for array in (rollout_map, row_counts, rows)])


def settle_kernel(skip, parts, flat, codes_ref, scales_ref, most, codes, out_sem):
    blocks = most.shape[0]

    def rows_of(b):
        return flat[pl.ds(pl.multiple_of(skip + b * BLOCK, 8), BLOCK), :]

    share = blocks // parts

    def largest(b, carry):
        most[pl.ds(b, 1), :] = jnp.max(jnp.abs(rows_of(b)), axis=0, keepdims=True)
        return carry

    lax.fori_loop(0, blocks, largest, 0, unroll=share)
    denom = jnp.max(most[...], axis=1, keepdims=True) + EPSILON
    wide = jnp.broadcast_to(denom, most.shape)
    at = lax.broadcasted_iota(jnp.int32, wide.shape, 0)
    lane = lax.broadcasted_iota(jnp.int32, wide.shape, 1)
    line = jnp.sum(jnp.where(at == lane, wide, 0.0), axis=0, keepdims=True)
    scales_ref[0] = (line / CODE_RANGE)[:, :blocks]
    most[...] = 1.0 / wide

    def divide(b, carry):
        rows = pl.ds(pl.multiple_of(b * BLOCK, BLOCK), BLOCK)
        codes[rows, :] = (rows_of(b) * most[pl.ds(b, 1), :]).astype(jnp.bfloat16)
        return carry

    def deliver(p):
        rows = pl.ds(p * share * BLOCK, share * BLOCK)
        return pltpu.make_async_copy(codes.at[rows], codes_ref.at[0, 0, rows], out_sem.at[p])

    for p in range(parts):
        lax.fori_loop(p * share, (p + 1) * share, divide, 0, unroll=share)
        deliver(p).start()
    for p in range(parts):
        deliver(p).wait()


def settle(flat, skip, height, name="settle"):
    blocks = height // BLOCK
    parts = 8 if blocks % 8 == 0 else 1
    return pl.pallas_call(
        functools.partial(settle_kernel, skip, parts),
        name=name,
        out_shape=(
            jax.ShapeDtypeStruct((1, 1, height, BLOCK), jnp.bfloat16),
            jax.ShapeDtypeStruct((1, 1, blocks), jnp.float32),
        ),
        in_specs=[pl.BlockSpec(memory_space=pltpu.VMEM)],
        out_specs=(pl.BlockSpec(memory_space=pltpu.HBM), pl.BlockSpec(memory_space=pltpu.VMEM)),
        scratch_shapes=[
            pltpu.VMEM((blocks, BLOCK), jnp.float32),
            pltpu.VMEM((height, BLOCK), jnp.bfloat16),
            pltpu.SemaphoreType.DMA((parts,)),
        ],
        compiler_params=pltpu.CompilerParams(vmem_limit_bytes=32 << 20),
    )(flat)


def on_device(height, trainer_rows, row_counts, rollout_map):
    cap = trainer_rows.shape[2]
    ny = lax.axis_size("ep")
    nx = trainer_rows.shape[3] // BLOCK // 2
    flat = exchange(trainer_rows, row_counts, rollout_map, height, ny, nx)
    return settle(flat, pages_back(row_counts.shape[2], cap, height) * cap, height)


def solution(mesh, height=7168):
    placed = (P("ep", None, "fsdp", None), P(), P())
    return jax.shard_map(
        functools.partial(on_device, height),
        mesh=mesh,
        in_specs=placed,
        out_specs=(P("ep", "fsdp", None, None), P("ep", "fsdp", None)),
        check_vma=False,
    )
```

time: 70.3 us -> 66.9 us (0.952)
  the two profiles are of different devices: /device:TPU:1 before, /device:TPU:42 now
where the time goes in v3:
time: 66.9 us; the launch traced here: 66.7 us
  Pallas kernels  66.1 us (99%)
    pallas_call x1, Pallas kernels, exchange(): pl.pallas_call(functools.partial(exchange_kernel, ny, nx, back, lag, rest...  63.9 us
    pallas_call x1, Pallas kernels, settle(): pl.pallas_call(functools.partial(settle_kernel, skip, parts), name=name,...  2.16 us

profile of v3, /device:TPU:42, one launch (start us, length us, event | category | flops | bytes accessed | tf_op | source)
XLA Modules:
  0.0 66.7 jit_solution(10373934844582144895)
XLA Ops:
  0.6 63.9 %exchange.1.flat = f32[8280,128]{1,0:T(8,128)S(1)} custom-call(s32[8,8]{1,0:T(8,128)} %map_hbm.1, s32[8,8,64]{2,1,0:T(8,128)} %counts_hbm.1, bf16[1,8,120,1024]{3,2,1,0:T(8,128)(2,1)} %rows_hbm.1), custom_call_target="tpu_custom_call" | custom-call | tf_op jit(solution)/shard_map/exchange/pallas_call | solution.py:248
  64.6 2.2 %settle.1 = (bf16[1,1,7168,128]{3,2,1,0:T(8,128)(2,1)}, f32[1,1,56]{2,1,0:T(1,128)}) custom-call(f32[8280,128]{1,0:T(8,128)S(1)} %exchange.1.flat), custom_call_target="tpu_custom_call" | custom-call | tf_op jit(solution)/shard_map/settle/pallas_call | solution.py:321

commit v4 on v3

--- a/solution.py
+++ b/solution.py
@@ -54,8 +54,7 @@
     fetch_counts = pltpu.make_async_copy(counts_hbm, counts_ref, in_sem.at[1])
     fetch_map.start()
     fetch_counts.start()
-    for q in range(chunks):
-        fetch_column(q).start()
+    fetch_column(0).start()
 
     barrier = pltpu.get_barrier_semaphore()
     for d in range(1, ny):
@@ -63,6 +62,9 @@
         pl.semaphore_signal(barrier, inc=1, device_id=((z + d) % ny * nxc + xc, y), device_id_type=MESH)
     for d in range(1, nxc):
         pl.semaphore_signal(barrier, inc=1, device_id=(z * nxc + (xc + d) % nxc, y), device_id_type=MESH)
+
+    for q in range(1, chunks):
+        fetch_column(q).start()
 
     def paired(i):
         return ((i + 1) // 2) * (1 - 2 * ((i + 1) % 2)) + ny

time: 66.9 us -> 66.9 us (level)
  the two profiles are of different devices: /device:TPU:42 before, /device:TPU:34 now
where the time goes in v4:
time: 66.9 us; the launch traced here: 66.4 us
  Pallas kernels  65.8 us (98%)
    pallas_call x1, Pallas kernels, exchange(): pl.pallas_call(functools.partial(exchange_kernel, ny, nx, back, lag, rest...  63.6 us
    pallas_call x1, Pallas kernels, settle(): pl.pallas_call(functools.partial(settle_kernel, skip, parts), name=name,...  2.16 us

profile of v4, /device:TPU:34, one launch (start us, length us, event | category | flops | bytes accessed | tf_op | source)
XLA Modules:
  0.0 66.4 jit_solution(14904361249640793542)
XLA Ops:
  0.6 63.6 %exchange.1.flat = f32[8280,128]{1,0:T(8,128)S(1)} custom-call(s32[8,8]{1,0:T(8,128)} %map_hbm.1, s32[8,8,64]{2,1,0:T(8,128)} %counts_hbm.1, bf16[1,8,120,1024]{3,2,1,0:T(8,128)(2,1)} %rows_hbm.1), custom_call_target="tpu_custom_call" | custom-call | tf_op jit(solution)/shard_map/exchange/pallas_call | solution.py:250
  64.3 2.2 %settle.1 = (bf16[1,1,7168,128]{3,2,1,0:T(8,128)(2,1)}, f32[1,1,56]{2,1,0:T(1,128)}) custom-call(f32[8280,128]{1,0:T(8,128)S(1)} %exchange.1.flat), custom_call_target="tpu_custom_call" | custom-call | tf_op jit(solution)/shard_map/settle/pallas_call | solution.py:323
